TPU v7x, 32 devices: a whole 2x2x4 slice. The times are simulated.
32 devices in a mesh: groups: 2 (over x), ctx: 16 (over z, y, core).
Axes of the slice: x: 2, y: 2, z: 4, core: 2. Of those that a mesh axis runs over, the one named last changes fastest.
Arguments:
- queries: bfloat16 [3072, 64, 576], P(('groups', 'ctx')), parts along dimension 0, may hold values from -400 to 400
- kv_latent: bfloat16 [3072, 576], P(('groups', 'ctx')), parts along dimension 0, may hold values from -6 to 6
- span_order: int32 [64], P('groups'), parts along dimension 0, may hold values from 0 to 31, as said below
Outputs:
- attended: bfloat16 [3072, 32768], P(('groups', 'ctx')), parts along dimension 0
There are 2 independent parts, one for each index of `groups`. A program takes and returns all parts, laid end to end along the dimension named above; each array names one. Nothing has to cross between parts.
Inputs may be any that keep to these rules, and one draw needn't show every extreme that they name: `span_order`: entries 2 d and 2 d + 1 are d and 31 - d in an order drawn for each d.
All inputs are finite; a program needn't handle non-finite values.
Results may differ from a plain program's by a relative error of at most 0.0047.
Values may be sent and summed in bfloat16 or wider, within the bound.
A program may use at most 64 MiB of HBM per device.

v0:
```python
import jax
import jax.numpy as jnp
from jax import lax
from jax.sharding import PartitionSpec as P

KEY_DIM = 128
ROPE_DIM = 64
LATENT = 512
WINDOW = 7


def shifted(value, axis, steps):
    count = lax.axis_size(axis)
    initial, last = (max(0, -steps), min(count, count - steps))
    return lax.ppermute(value, axis, [(source, source + steps) for source in range(initial, last)])


def local(queries, kv_latent, span_order):
    devices = lax.axis_size("ctx")
    index = lax.axis_index("ctx")
    span = queries.shape[0] // 2
    own_ids = lax.dynamic_slice_in_dim(span_order, 2 * index, 2)
    lower_first = own_ids[0] < devices
    earlier = jnp.where(lower_first, kv_latent[:span], kv_latent[span:])
    ahead = [shifted(earlier, "ctx", step) for step in range(1, WINDOW + 1)]
    behind = [shifted(kv_latent, "ctx", -step) for step in range(1, WINDOW + 1)]
    source = jnp.concatenate(ahead + [kv_latent] + behind, axis=0)
    width = (WINDOW + 1) * span
    scale = (KEY_DIM + ROPE_DIM) ** (-0.5)
    rows = jnp.arange(span, dtype=jnp.int32)
    keypos = jnp.arange(width, dtype=jnp.int32)
    backs = WINDOW - keypos // span
    query_slots = queries.reshape(2, span, queries.shape[1], queries.shape[2])
    outputs = []
    for slot in range(2):
        span_id = own_ids[slot]
        picked = []
        for back in range(WINDOW, -1, -1):
            wanted = jnp.maximum(span_id - back, 0)
            holder = jnp.where(wanted < devices, wanted, 2 * devices - 1 - wanted)
            holder_ids = lax.dynamic_slice_in_dim(span_order, 2 * holder, 2)
            second = jnp.where(holder_ids[0] == wanted, 0, 1)
            offset = holder - index
            block = jnp.where(offset < 0, -offset - 1, WINDOW + 2 * offset + second)
            picked.append(
                lax.dynamic_slice_in_dim(source, jnp.clip(block, 0, 3 * WINDOW + 1) * span, span, 0)
            )
        window = jnp.concatenate(picked, axis=0)
        scores = (
            jnp.einsum("phl,kl->hpk", query_slots[slot], window, preferred_element_type=jnp.float32)
            * scale
        )
        allowed = (span_id - backs >= 0)[None, :] & (
            (backs > 0)[None, :] | ((keypos % span)[None, :] <= rows[:, None])
        )
        scores = jnp.where(allowed[None], scores, -1e30)
        largest = jnp.max(scores, axis=-1, keepdims=True)
        weights = jnp.where(allowed[None], jnp.exp(scores - largest), 0.0)
        probs = (weights / jnp.sum(weights, axis=-1, keepdims=True)).astype(jnp.bfloat16)
        mixed = jnp.einsum(
            "hpk,kl->phl", probs, window[:, :LATENT], preferred_element_type=jnp.float32
        ).astype(jnp.bfloat16)
        outputs.append(mixed.reshape(span, queries.shape[1] * LATENT))
    return jnp.concatenate(outputs, axis=0)


def solution(mesh):
    in_specs = (P(("groups", "ctx"), None, None), P(("groups", "ctx"), None), P("groups"))
    out_specs = P(("groups", "ctx"), None)
    return jax.shard_map(local, mesh=mesh, in_specs=in_specs, out_specs=out_specs, check_vma=False)
```

profile of v0, /device:TPU:1, one launch (start us, length us, event | category | flops | bytes accessed | tf_op | source)
XLA Modules:
  0.0 109.5 jit_solution(17485401193482374685)
XLA Ops:
  3.1 5.6 %collective-permute-start.6 = (bf16[48,576]{0,1:T(8,128)(2,1)S(1)}, bf16[48,576]{0,1:T(8,128)(2,1)S(1)}, u32[]{:S(2)}, u32[]{:S(2)}) collective-permute-start(bf16[48,576]{0,1:T(8,128)(2,1)S(1)} %slice_select_fusion), channel_id=1, source_target_pairs={{0,7},{1,8},{2,9},{3,10},{4,11},{5,12},{6,13},{7,14},{8,15},{16,23... | collective-permute-start | bytes 165896 | tf_op jit(solution)/shard_map/ppermute | solution.py:15
  8.7 4.2 %collective-permute-start.5 = (bf16[48,576]{0,1:T(8,128)(2,1)S(1)}, bf16[48,576]{0,1:T(8,128)(2,1)S(1)}, u32[]{:S(2)}, u32[]{:S(2)}) collective-permute-start(bf16[48,576]{0,1:T(8,128)(2,1)S(1)} %slice_select_fusion), channel_id=1, source_target_pairs={{0,6},{1,7},{2,8},{3,9},{4,10},{5,11},{6,12},{7,13},{8,14},{9,15},... | collective-permute-start | bytes 165896 | tf_op jit(solution)/shard_map/ppermute | solution.py:15
  12.9 1.6 %collective-permute-start.4 = (bf16[48,576]{0,1:T(8,128)(2,1)S(1)}, bf16[48,576]{0,1:T(8,128)(2,1)S(1)}, u32[]{:S(2)}, u32[]{:S(2)}) collective-permute-start(bf16[48,576]{0,1:T(8,128)(2,1)S(1)} %slice_select_fusion), channel_id=1, source_target_pairs={{0,5},{1,6},{2,7},{3,8},{4,9},{5,10},{6,11},{7,12},{8,13},{9,14},{... | collective-permute-start | bytes 165896 | tf_op jit(solution)/shard_map/ppermute | solution.py:15
  14.5 1.3 %collective-permute-start.3 = (bf16[48,576]{0,1:T(8,128)(2,1)S(1)}, bf16[48,576]{0,1:T(8,128)(2,1)S(1)}, u32[]{:S(2)}, u32[]{:S(2)}) collective-permute-start(bf16[48,576]{0,1:T(8,128)(2,1)S(1)} %slice_select_fusion), channel_id=1, source_target_pairs={{0,4},{1,5},{2,6},{3,7},{4,8},{5,9},{6,10},{7,11},{8,12},{9,13},{1... | collective-permute-start | bytes 165896 | tf_op jit(solution)/shard_map/ppermute | solution.py:15
  15.8 3.1 %collective-permute-start.2 = (bf16[48,576]{0,1:T(8,128)(2,1)S(1)}, bf16[48,576]{0,1:T(8,128)(2,1)S(1)}, u32[]{:S(2)}, u32[]{:S(2)}) collective-permute-start(bf16[48,576]{0,1:T(8,128)(2,1)S(1)} %slice_select_fusion), channel_id=1, source_target_pairs={{0,3},{1,4},{2,5},{3,6},{4,7},{5,8},{6,9},{7,10},{8,11},{9,12},{10... | collective-permute-start | bytes 165896 | tf_op jit(solution)/shard_map/ppermute | solution.py:15
  20.2 1.9 %collective-permute-start.1 = (bf16[48,576]{0,1:T(8,128)(2,1)S(1)}, bf16[48,576]{0,1:T(8,128)(2,1)S(1)}, u32[]{:S(2)}, u32[]{:S(2)}) collective-permute-start(bf16[48,576]{0,1:T(8,128)(2,1)S(1)} %slice_select_fusion), channel_id=1, source_target_pairs={{0,2},{1,3},{2,4},{3,5},{4,6},{5,7},{6,8},{7,9},{8,10},{9,11},{10,... | collective-permute-start | bytes 165896 | tf_op jit(solution)/shard_map/ppermute | solution.py:15
  22.1 3.6 %collective-permute-start = (bf16[48,576]{0,1:T(8,128)(2,1)S(1)}, bf16[48,576]{0,1:T(8,128)(2,1)S(1)}, u32[]{:S(2)}, u32[]{:S(2)}) collective-permute-start(bf16[48,576]{0,1:T(8,128)(2,1)S(1)} %slice_select_fusion), channel_id=1, source_target_pairs={{0,1},{1,2},{2,3},{3,4},{4,5},{5,6},{6,7},{7,8},{8,9},{9,10},{10,1... | collective-permute-start | bytes 165896 | tf_op jit(solution)/shard_map/ppermute | solution.py:15
  25.8 1.3 %collective-permute-start.12 = (bf16[96,576]{0,1:T(8,128)(2,1)S(1)}, bf16[96,576]{0,1:T(8,128)(2,1)S(1)}, u32[]{:S(2)}, u32[]{:S(2)}) collective-permute-start(bf16[96,576]{0,1:T(8,128)(2,1)S(1)} %copy.4), channel_id=1, source_target_pairs={{6,0},{7,1},{8,2},{9,3},{10,4},{11,5},{12,6},{13,7},{14,8},{15,9},... | collective-permute-start | bytes 331784 | tf_op jit(solution)/shard_map/ppermute | solution.py:15
  42.8 1.9 %collective-permute-start.7 = (bf16[96,576]{0,1:T(8,128)(2,1)S(1)}, bf16[96,576]{0,1:T(8,128)(2,1)S(1)}, u32[]{:S(2)}, u32[]{:S(2)}) collective-permute-start(bf16[96,576]{0,1:T(8,128)(2,1)S(1)} %copy.4), channel_id=1, source_target_pairs={{1,0},{2,1},{3,2},{4,3},{5,4},{6,5},{7,6},{8,7},{9,8},{10,9},{11,1... | collective-permute-start | bytes 331784 | tf_op jit(solution)/shard_map/ppermute | solution.py:15
  46.0 1.4 %fusion.37 = (s32[2]{0:T(128)S(1)}, s32[2]{0:T(128)S(1)}, s32[2]{0:T(128)S(1)}, s32[2]{0:T(128)S(1)}, s32[2]{0:T(128)S(1)}, /*index=5*/s32[2]{0:T(128)S(1)}, s32...) fusion(s32[32]{0:T(128)} %param.5, ...), kind=kLoop, calls=%fused_computation.71 | loop fusion | bytes 320 | tf_op jit(solution)/shard_map/dynamic_slice | solution.py:41
  48.6 2.7 %collective-permute-done.8 = bf16[96,576]{0,1:T(8,128)(2,1)S(1)} collective-permute-done((bf16[96,576]{0,1:T(8,128)(2,1)S(1)}, bf16[96,576]{0,1:T(8,128)(2,1)S(1)}, u32[]{:S(2)}, u32[]{:S(2)}) %collective-permute-start.8) | collective-permute-done | bytes 110624 | tf_op jit(solution)/shard_map/ppermute | solution.py:15
  51.4 13.5 %collective-permute-done.13 = bf16[96,576]{0,1:T(8,128)(2,1)S(1)} collective-permute-done((bf16[96,576]{0,1:T(8,128)(2,1)S(1)}, bf16[96,576]{0,1:T(8,128)(2,1)S(1)}, u32[]{:S(2)}, u32[]{:S(2)}) %collective-permute-start.13) | collective-permute-done | bytes 110624 | tf_op jit(solution)/shard_map/ppermute | solution.py:15
  64.8 1.3 %concatenate.12 = bf16[1104,576]{0,1:T(8,128)(2,1)S(1)} concatenate(bf16[48,576]{0,1:T(8,128)(2,1)S(1)} %collective-permute-done, bf16[48,576]{0,1:T(8,128)(2,1)S(1)} %collective-permute-done.1, bf16[48,576]{0,1:T(8,128)(2,1)S(1)} %collective-permute-done.2, bf16[48,576]{0,1:T(8,128)(2,1)S(1)} %collective-permute-done.3, bf16[48,576]{0,1:T(8,128)(2,1)S(1)} %collective-permute-done.4, ...), dimensions={0} | concatenate | bytes 2543616 | tf_op jit(solution)/shard_map/concatenate | solution.py:27
  66.2 2.3 %constant_dynamic-slice_fusion.8 = (bf16[48,576]{0,1:T(8,128)(2,1)S(1)}, bf16[48,576]{0,1:T(8,128)(2,1)S(1)}, bf16[48,576]{0,1:T(8,128)(2,1)S(1)}, bf16[48,576]{...) fusion(bf16[1104,576]{0,1:T(8,128)(2,1)S(1)} %concatenate.12, ...), kind=kLoop, calls=%fused_computation.51 | loop fusion | bytes 1769536 | tf_op jit(solution)/shard_map/dynamic_slice | solution.py:46
  69.1 4.5 %fusion.2 = f32[384,48,64]{0,2,1:T(8,128)S(1)} fusion(bf16[96,64,576]{2,1,0:T(8,128)(2,1)} %param.3, bf16[384,576]{0,1:T(8,128)(2,1)S(1)} %concatenate.14), kind=kOutput, calls=%fused_computation.9 | convolution fusion | flops 1358954496 | bytes 9093120 | tf_op jit(solution)/shard_map/phl,kl->hpk/dot_general | solution.py:50
  73.7 8.8 %fusion.39 = (f32[64,48]{0,1:T(8,128)S(1)}, f32[64,48,384]{2,0,1:T(8,128)S(1)}) fusion(f32[384,48,64]{0,2,1:T(8,128)S(1)} %fusion.2, pred[48,384]{1,0:T(8,128)(4,1)S(1)} %copy-done.2), kind=kOutput, calls=%fused_computation.73 | output fusion | flops 8257919 | bytes 9467904 | tf_op jit(solution)/shard_map/sub | solution.py:58
  82.5 2.1 %fusion.18 = bf16[512,64,48]{0,1,2:T(8,128)(2,1)S(1)} fusion(f32[64,48,384]{2,0,1:T(8,128)S(1)} %get-tuple-element.42, f32[64,48]{0,1:T(8,128)S(1)} %get-tuple-element.41, bf16[384,576]{0,1:T(8,128)(2,1)S(1)} %concatenate.14), kind=kOutput, calls=%fused_computation.25 | convolution fusion | flops 1211891712 | bytes 8282112 | tf_op jit(solution)/shard_map/hpk,kl->phl/dot_general | solution.py:60
  84.6 1.9 %copy.21 = bf16[6,8,64,512]{3,1,2,0:T(8,128)(2,1)S(1)} copy(bf16[6,8,64,512]{3,2,1,0:T(8,128)(2,1)S(1)} %bitcast.76) | data formatting | bytes 6291456
  86.5 2.3 %concatenate.13 = bf16[384,576]{0,1:T(8,128)(2,1)} concatenate(bf16[48,576]{0,1:T(8,128)(2,1)} %get-tuple-element.20, bf16[48,576]{0,1:T(8,128)(2,1)} %get-tuple-element.19, bf16[48,576]{0,1:T(8,128)(2,1)} %get-tuple-element.18, bf16[48,576]{0,1:T(8,128)(2,1)} %get-tuple-element.17, bf16[48,576]{0,1:T(8,128)(2,1)} %get-tuple-element.16, bf16[48,576]{0,1:T(8,128)(2,1)} %get-tuple-element.15, ...), dimensions={0} | concatenate | bytes 884736 | tf_op jit(solution)/shard_map/concatenate | solution.py:48
  88.8 4.7 %fusion.4 = f32[384,48,64]{0,2,1:T(8,128)S(1)} fusion(bf16[96,64,576]{2,1,0:T(8,128)(2,1)} %param.3, bf16[384,576]{0,1:T(8,128)(2,1)} %concatenate.13), kind=kOutput, calls=%fused_computation.11 | convolution fusion | flops 1358954496 | bytes 9093120 | tf_op jit(solution)/shard_map/phl,kl->hpk/dot_general | solution.py:50
  93.5 8.8 %fusion.40 = (f32[64,48]{0,1:T(8,128)S(1)}, f32[64,48,384]{2,0,1:T(8,128)S(1)}) fusion(f32[384,48,64]{0,2,1:T(8,128)S(1)} %fusion.4, pred[48,384]{1,0:T(8,128)(4,1)S(1)} %copy-done.1), kind=kOutput, calls=%fused_computation.74 | output fusion | flops 8257919 | bytes 9467904 | tf_op jit(solution)/shard_map/sub | solution.py:58
  102.4 2.2 %fusion.19 = bf16[512,64,48]{0,1,2:T(8,128)(2,1)S(1)} fusion(f32[64,48,384]{2,0,1:T(8,128)S(1)} %get-tuple-element.44, f32[64,48]{0,1:T(8,128)S(1)} %get-tuple-element.43, bf16[384,576]{0,1:T(8,128)(2,1)S(1)} %copy-done), kind=kOutput, calls=%fused_computation.26 | convolution fusion | flops 1211891712 | bytes 8282112 | tf_op jit(solution)/shard_map/hpk,kl->phl/dot_general | solution.py:60
  104.5 1.8 %copy.20 = bf16[6,8,64,512]{3,1,2,0:T(8,128)(2,1)S(1)} copy(bf16[6,8,64,512]{3,2,1,0:T(8,128)(2,1)S(1)} %bitcast.77) | data formatting | bytes 6291456
  106.4 3.1 %pad_maximum_fusion = bf16[96,32768]{1,0:T(8,128)(2,1)} fusion(bf16[48,32768]{1,0:T(8,128)(2,1)S(1)} %bitcast.74, bf16[48,32768]{1,0:T(8,128)(2,1)S(1)} %bitcast.75), kind=kLoop, calls=%fused_computation.2 | loop fusion | flops 12582912 | bytes 12582912 | tf_op jit(solution)/shard_map/concatenate | solution.py:64
  (32 shorter events, 11.8 us)
Async XLA Ops:
  3.1 17.1 %collective-permute-start.6 = (bf16[48,576]{0,1:T(8,128)(2,1)S(1)}, bf16[48,576]{0,1:T(8,128)(2,1)S(1)}, u32[]{:S(2)}, u32[]{:S(2)}) collective-permute-start(bf16[48,576]{0,1:T(8,128)(2,1)S(1)} %slice_select_fusion), channel_id=1, source_target_pairs={{0,7},{1,8},{2,9},{3,10},{4,11},{5,12},{6,13},{7,14},{8,15},{16,23... | collective-permute-start | bytes 165896 | tf_op jit(solution)/shard_map/ppermute | solution.py:15
  8.7 13.4 %collective-permute-start.5 = (bf16[48,576]{0,1:T(8,128)(2,1)S(1)}, bf16[48,576]{0,1:T(8,128)(2,1)S(1)}, u32[]{:S(2)}, u32[]{:S(2)}) collective-permute-start(bf16[48,576]{0,1:T(8,128)(2,1)S(1)} %slice_select_fusion), channel_id=1, source_target_pairs={{0,6},{1,7},{2,8},{3,9},{4,10},{5,11},{6,12},{7,13},{8,14},{9,15},... | collective-permute-start | bytes 165896 | tf_op jit(solution)/shard_map/ppermute | solution.py:15
  12.9 12.9 %collective-permute-start.4 = (bf16[48,576]{0,1:T(8,128)(2,1)S(1)}, bf16[48,576]{0,1:T(8,128)(2,1)S(1)}, u32[]{:S(2)}, u32[]{:S(2)}) collective-permute-start(bf16[48,576]{0,1:T(8,128)(2,1)S(1)} %slice_select_fusion), channel_id=1, source_target_pairs={{0,5},{1,6},{2,7},{3,8},{4,9},{5,10},{6,11},{7,12},{8,13},{9,14},{... | collective-permute-start | bytes 165896 | tf_op jit(solution)/shard_map/ppermute | solution.py:15
  14.5 12.6 %collective-permute-start.3 = (bf16[48,576]{0,1:T(8,128)(2,1)S(1)}, bf16[48,576]{0,1:T(8,128)(2,1)S(1)}, u32[]{:S(2)}, u32[]{:S(2)}) collective-permute-start(bf16[48,576]{0,1:T(8,128)(2,1)S(1)} %slice_select_fusion), channel_id=1, source_target_pairs={{0,4},{1,5},{2,6},{3,7},{4,8},{5,9},{6,10},{7,11},{8,12},{9,13},{1... | collective-permute-start | bytes 165896 | tf_op jit(solution)/shard_map/ppermute | solution.py:15
  15.8 23.1 %collective-permute-start.2 = (bf16[48,576]{0,1:T(8,128)(2,1)S(1)}, bf16[48,576]{0,1:T(8,128)(2,1)S(1)}, u32[]{:S(2)}, u32[]{:S(2)}) collective-permute-start(bf16[48,576]{0,1:T(8,128)(2,1)S(1)} %slice_select_fusion), channel_id=1, source_target_pairs={{0,3},{1,4},{2,5},{3,6},{4,7},{5,8},{6,9},{7,10},{8,11},{9,12},{10... | collective-permute-start | bytes 165896 | tf_op jit(solution)/shard_map/ppermute | solution.py:15
  20.2 20.0 %collective-permute-start.1 = (bf16[48,576]{0,1:T(8,128)(2,1)S(1)}, bf16[48,576]{0,1:T(8,128)(2,1)S(1)}, u32[]{:S(2)}, u32[]{:S(2)}) collective-permute-start(bf16[48,576]{0,1:T(8,128)(2,1)S(1)} %slice_select_fusion), channel_id=1, source_target_pairs={{0,2},{1,3},{2,4},{3,5},{4,6},{5,7},{6,8},{7,9},{8,10},{9,11},{10,... | collective-permute-start | bytes 165896 | tf_op jit(solution)/shard_map/ppermute | solution.py:15
  22.1 19.4 %collective-permute-start = (bf16[48,576]{0,1:T(8,128)(2,1)S(1)}, bf16[48,576]{0,1:T(8,128)(2,1)S(1)}, u32[]{:S(2)}, u32[]{:S(2)}) collective-permute-start(bf16[48,576]{0,1:T(8,128)(2,1)S(1)} %slice_select_fusion), channel_id=1, source_target_pairs={{0,1},{1,2},{2,3},{3,4},{4,5},{5,6},{6,7},{7,8},{8,9},{9,10},{10,1... | collective-permute-start | bytes 165896 | tf_op jit(solution)/shard_map/ppermute | solution.py:15
  25.8 17.0 %collective-permute-start.12 = (bf16[96,576]{0,1:T(8,128)(2,1)S(1)}, bf16[96,576]{0,1:T(8,128)(2,1)S(1)}, u32[]{:S(2)}, u32[]{:S(2)}) collective-permute-start(bf16[96,576]{0,1:T(8,128)(2,1)S(1)} %copy.4), channel_id=1, source_target_pairs={{6,0},{7,1},{8,2},{9,3},{10,4},{11,5},{12,6},{13,7},{14,8},{15,9},... | collective-permute-start | bytes 331784 | tf_op jit(solution)/shard_map/ppermute | solution.py:15
  27.1 17.6 %collective-permute-start.11 = (bf16[96,576]{0,1:T(8,128)(2,1)S(1)}, bf16[96,576]{0,1:T(8,128)(2,1)S(1)}, u32[]{:S(2)}, u32[]{:S(2)}) collective-permute-start(bf16[96,576]{0,1:T(8,128)(2,1)S(1)} %copy.4), channel_id=1, source_target_pairs={{5,0},{6,1},{7,2},{8,3},{9,4},{10,5},{11,6},{12,7},{13,8},{14,9},{... | collective-permute-start | bytes 331784 | tf_op jit(solution)/shard_map/ppermute | solution.py:15
  38.9 9.5 %collective-permute-start.10 = (bf16[96,576]{0,1:T(8,128)(2,1)S(1)}, bf16[96,576]{0,1:T(8,128)(2,1)S(1)}, u32[]{:S(2)}, u32[]{:S(2)}) collective-permute-start(bf16[96,576]{0,1:T(8,128)(2,1)S(1)} %copy.4), channel_id=1, source_target_pairs={{4,0},{5,1},{6,2},{7,3},{8,4},{9,5},{10,6},{11,7},{12,8},{13,9},{1... | collective-permute-start | bytes 331784 | tf_op jit(solution)/shard_map/ppermute | solution.py:15
  40.2 8.5 %collective-permute-start.9 = (bf16[96,576]{0,1:T(8,128)(2,1)S(1)}, bf16[96,576]{0,1:T(8,128)(2,1)S(1)}, u32[]{:S(2)}, u32[]{:S(2)}) collective-permute-start(bf16[96,576]{0,1:T(8,128)(2,1)S(1)} %copy.4), channel_id=1, source_target_pairs={{3,0},{4,1},{5,2},{6,3},{7,4},{8,5},{9,6},{10,7},{11,8},{12,9},{13... | collective-permute-start | bytes 331784 | tf_op jit(solution)/shard_map/ppermute | solution.py:15
  41.5 9.9 %collective-permute-start.8 = (bf16[96,576]{0,1:T(8,128)(2,1)S(1)}, bf16[96,576]{0,1:T(8,128)(2,1)S(1)}, u32[]{:S(2)}, u32[]{:S(2)}) collective-permute-start(bf16[96,576]{0,1:T(8,128)(2,1)S(1)} %copy.4), channel_id=1, source_target_pairs={{2,0},{3,1},{4,2},{5,3},{6,4},{7,5},{8,6},{9,7},{10,8},{11,9},{12,... | collective-permute-start | bytes 331784 | tf_op jit(solution)/shard_map/ppermute | solution.py:15
  42.8 8.6 %collective-permute-start.7 = (bf16[96,576]{0,1:T(8,128)(2,1)S(1)}, bf16[96,576]{0,1:T(8,128)(2,1)S(1)}, u32[]{:S(2)}, u32[]{:S(2)}) collective-permute-start(bf16[96,576]{0,1:T(8,128)(2,1)S(1)} %copy.4), channel_id=1, source_target_pairs={{1,0},{2,1},{3,2},{4,3},{5,4},{6,5},{7,6},{8,7},{9,8},{10,9},{11,1... | collective-permute-start | bytes 331784 | tf_op jit(solution)/shard_map/ppermute | solution.py:15
  44.7 20.1 %collective-permute-start.13 = (bf16[96,576]{0,1:T(8,128)(2,1)S(1)}, bf16[96,576]{0,1:T(8,128)(2,1)S(1)}, u32[]{:S(2)}, u32[]{:S(2)}) collective-permute-start(bf16[96,576]{0,1:T(8,128)(2,1)S(1)} %copy.4), channel_id=1, source_target_pairs={{7,0},{8,1},{9,2},{10,3},{11,4},{12,5},{13,6},{14,7},{15,8},{23,16... | collective-permute-start | bytes 331784 | tf_op jit(solution)/shard_map/ppermute | solution.py:15
  69.1 4.5 %copy-start.2 = (pred[48,384]{1,0:T(8,128)(4,1)S(1)}, pred[48,384]{1,0:T(8,128)(4,1)}, u32[]{:S(2)}) copy-start(pred[48,384]{1,0:T(8,128)(4,1)} %get-tuple-element.22) | copy-start | bytes 55300
  88.8 4.8 %copy-start.1 = (pred[48,384]{1,0:T(8,128)(4,1)S(1)}, pred[48,384]{1,0:T(8,128)(4,1)}, u32[]{:S(2)}) copy-start(pred[48,384]{1,0:T(8,128)(4,1)} %get-tuple-element.21) | copy-start | bytes 55300
  93.5 8.8 %copy-start = (bf16[384,576]{0,1:T(8,128)(2,1)S(1)}, bf16[384,576]{0,1:T(8,128)(2,1)}, u32[]{:S(2)}) copy-start(bf16[384,576]{0,1:T(8,128)(2,1)} %concatenate.13) | copy-start | bytes 1327108
where the time goes:
time: 110 us
  starting transfers between devices  31 us (28%)
  other arithmetic  22.7 us (21%)
  waiting for transfers between devices  16.5 us (15%)
  local copies, waits for them, and re-layouts  14 us (13%)
  matrix products  13.6 us (12%)
  between operations  11.7 us (11%)
    ppermute x14, starting transfers between devices, shifted(): lax.ppermute(value, axis, [(source, source + steps) for source in range(i...  31 us
    sub x2, other arithmetic, local(): weights = jnp.where(allowed[None], jnp.exp(scores - largest), 0.0)  17.6 us
    ppermute x14, waiting for transfers between devices, shifted(): lax.ppermute(value, axis, [(source, source + steps) for source in range(i...  16.5 us
    dot_general x2, matrix products, local(): jnp.einsum('phl,kl->hpk', query_slots[slot], window, preferred_element_ty...  9.27 us
    unnamed x9, local copies, waits for them, and re-layouts  4.75 us
    dot_general x2, matrix products, local(): jnp.einsum('hpk,kl->phl', probs, window[:, :LATENT], preferred_element_ty...  4.29 us
    concatenate x1, other arithmetic, local(): return jnp.concatenate(outputs, axis=0)  3.14 us
    concatenate x2, local copies, waits for them, and re-layouts, local(): window = jnp.concatenate(picked, axis=0)  2.93 us
  transfers between devices with their start and end apart: 14, of which 3 were waited for; matrix products, arithmetic and copies ran while one was open for 3% of the time, Pallas kernels for 0%

commit v1 on v0

v1 whole, which is shorter than its diff:
```python
import functools

import jax
import jax.numpy as jnp
from jax import lax
from jax.experimental import pallas as pl
from jax.experimental.pallas import tpu as pltpu
from jax.sharding import PartitionSpec as P

KEY_DIM = 128
ROPE_DIM = 64
LATENT = 512
WINDOW = 7
HEAD_BLOCK = 16
LOG2E = 1.4426950408889634
MESH = pl.DeviceIdType.MESH


def gather_kernel(n, span, order_ref, kv_ref, win_ref, mine, send_lo, send_hi, send_x, recv_sem):
    me = lax.axis_index("ctx")
    last = 2 * n - 1

    barrier = pltpu.get_barrier_semaphore()
    for k in range(1, WINDOW + 1):
        for other, ok in ((me + k, me + k < n), (me - k, me >= k)):
            @pl.when(ok)
            def _():
                pl.semaphore_signal(barrier, inc=1, device_id={"ctx": other}, device_id_type=MESH)

    first, second = kv_ref[:span], kv_ref[span:]
    lower_first = jnp.full(first.shape, order_ref[2 * me], jnp.int32) < n
    own_lower = jnp.where(lower_first, first, second)
    own_upper = jnp.where(lower_first, second, first)
    mine[0] = own_lower
    mine[1] = own_upper
    own_rows = pl.ds(WINDOW * span, span)
    pl.semaphore_wait(barrier, jnp.minimum(me, WINDOW) + jnp.minimum(n - 1 - me, WINDOW))

    def rows(back):
        return pl.ds(pl.multiple_of((WINDOW - back) * span, 16), span)

    def copy(which, target, window, back, send):
        return pltpu.make_async_remote_copy(
            src_ref=mine.at[which],
            dst_ref=win_ref.at[window, rows(back)],
            send_sem=send,
            recv_sem=recv_sem.at[window, back],
            device_id={"ctx": target},
            device_id_type=MESH,
        )

    def sends(action):
        for k in range(1, WINDOW + 1):
            @pl.when(me + k < n)
            def _():
                action(copy(0, me + k, 0, k, send_lo.at[k]))

            @pl.when(me >= k)
            def _():
                action(copy(1, me - k, 1, k, send_hi.at[k]))

            back = last - 2 * me + k

            @pl.when((me >= k) & (back <= WINDOW))
            def _():
                action(copy(0, me - k, 1, back, send_x.at[k]))

    sends(lambda c: c.start())
    win_ref[0, own_rows] = own_lower
    win_ref[1, own_rows] = own_upper
    for k in range(1, WINDOW + 1):
        @pl.when(me >= k)
        def _():
            copy(0, me - k, 0, k, send_lo.at[k]).wait_recv()

        @pl.when(me < k)
        def _():
            win_ref[0, rows(k)] = jnp.zeros_like(own_lower)

    for k in range(1, WINDOW + 1):
        @pl.when(2 * me + k < last)
        def _():
            copy(0, jnp.where(me + 1 < n, me + 1, me - 1), 1, k, send_lo.at[k]).wait_recv()

        @pl.when(2 * me + k >= last)
        def _():
            win_ref[1, rows(k)] = win_ref[0, rows(2 * me + k - last)]
    sends(lambda c: c.wait_send())


def attend_kernel(n, span, heads, order_ref, q_ref, win_ref, out_ref, scores, bias, probs):
    slot, group = pl.program_id(0), pl.program_id(1)
    me = order_ref[order_ref.shape[0] - 1]
    width = (WINDOW + 1) * span
    span_id = order_ref[2 * me + slot]
    factor = LOG2E * (KEY_DIM + ROPE_DIM) ** -0.5

    @pl.when(group == 0)
    def _():
        keypos = lax.broadcasted_iota(jnp.int32, (span, width), 1)
        row = lax.broadcasted_iota(jnp.int32, (span, width), 0)
        allowed = (keypos >= (WINDOW - span_id) * span) & (keypos - WINDOW * span <= row)
        bias[...] = jnp.where(allowed, 0.0, -1e30)

    block = q_ref[...].reshape(span * HEAD_BLOCK, q_ref.shape[2])
    product = lax.dot_general(block, win_ref[0], (((1,), (1,)), ((), ())), preferred_element_type=jnp.float32)
    chunks = width // 128
    for c in range(chunks):
        scores[c] = product[:, c * 128 : (c + 1) * 128]
    for h in range(HEAD_BLOCK):
        parts = [
            scores.at[c][pl.ds(h, span, stride=HEAD_BLOCK), :] + bias[:, c * 128 : (c + 1) * 128]
            for c in range(chunks)
        ]
        largest = jnp.max(functools.reduce(jnp.maximum, parts), axis=-1, keepdims=True)
        weights = [jnp.exp2((part - largest) * factor) for part in parts]
        inverse = 1.0 / jnp.sum(sum(weights), axis=-1, keepdims=True)
        for c in range(chunks):
            probs[h * span : (h + 1) * span, c * 128 : (c + 1) * 128] = (weights[c] * inverse).astype(jnp.bfloat16)
    mixed = jnp.dot(probs[...], win_ref[0, :, :LATENT], preferred_element_type=jnp.float32)
    for h in range(HEAD_BLOCK):
        out_ref[:, h * LATENT : (h + 1) * LATENT] = mixed[h * span : (h + 1) * span].astype(jnp.bfloat16)


def local(queries, kv_latent, span_order):
    n = lax.axis_size("ctx")
    tokens, heads, dim = queries.shape
    span = tokens // 2
    width = (WINDOW + 1) * span
    windows = pl.pallas_call(
        functools.partial(gather_kernel, n, span),
        out_shape=jax.ShapeDtypeStruct((2, width, dim), jnp.bfloat16),
        in_specs=[pl.BlockSpec(memory_space=pltpu.SMEM), pl.BlockSpec(memory_space=pltpu.VMEM)],
        out_specs=pl.BlockSpec(memory_space=pltpu.VMEM),
        scratch_shapes=[
            pltpu.VMEM((2, span, dim), jnp.bfloat16),
            pltpu.SemaphoreType.DMA((WINDOW + 1,)),
            pltpu.SemaphoreType.DMA((WINDOW + 1,)),
            pltpu.SemaphoreType.DMA((WINDOW + 1,)),
            pltpu.SemaphoreType.DMA((2, WINDOW + 1)),
        ],
        compiler_params=pltpu.CompilerParams(collective_id=0, has_side_effects=True),
        name="gather_windows",
    )(span_order, kv_latent)
    scalars = jnp.concatenate([span_order, lax.axis_index("ctx")[None].astype(jnp.int32)])

    def window_of(slot, group, order):
        return jnp.where(order[2 * order[2 * n] + slot] < n, 0, 1), 0, 0

    return pl.pallas_call(
        functools.partial(attend_kernel, n, span, heads),
        out_shape=jax.ShapeDtypeStruct((tokens, heads * LATENT), jnp.bfloat16),
        grid_spec=pltpu.PrefetchScalarGridSpec(
            num_scalar_prefetch=1,
            grid=(2, heads // HEAD_BLOCK),
            in_specs=[
                pl.BlockSpec((span, HEAD_BLOCK, dim), lambda s, g, order: (s, g, 0)),
                pl.BlockSpec((1, width, dim), window_of),
            ],
            out_specs=pl.BlockSpec((span, HEAD_BLOCK * LATENT), lambda s, g, order: (s, g)),
            scratch_shapes=[
                pltpu.VMEM((width // 128, span * HEAD_BLOCK, 128), jnp.float32),
                pltpu.VMEM((span, width), jnp.float32),
                pltpu.VMEM((span * HEAD_BLOCK, width), jnp.bfloat16),
            ],
        ),
        compiler_params=pltpu.CompilerParams(vmem_limit_bytes=48 * 1024 * 1024),
        name="attend",
    )(scalars, queries, windows)


def solution(mesh):
    in_specs = (P(("groups", "ctx"), None, None), P(("groups", "ctx"), None), P("groups"))
    out_specs = P(("groups", "ctx"), None)
    return jax.shard_map(local, mesh=mesh, in_specs=in_specs, out_specs=out_specs, check_vma=False)
```

time: 110 us -> 41.2 us (0.37)
  Pallas kernels: 0 us -> 39 us
  starting transfers between devices: 31 us -> 0 us
  other arithmetic: 22.7 us -> 0.73 us
  waiting for transfers between devices: 16.5 us -> 0 us
  matrix products: 13.6 us -> 0 us
  local copies, waits for them, and re-layouts: 14 us -> 1.19 us
  between operations: 11.7 us -> 0.02 us
    pallas_call x0 -> x2, Pallas kernels: none -> 39 us  [the longest x1 21.1 us: local(): pl.pallas_call(functools.partial(gather_kernel, n, span), out_shape=jax.S...]
    ppermute x14 -> x0, starting transfers between devices: 31 us -> none  [shifted(): lax.ppermute(value, axis, [(source, source + steps) for source in range(i...]
    sub x2 -> x0, other arithmetic: 17.6 us -> none  [local(): weights = jnp.where(allowed[None], jnp.exp(scores - largest), 0.0)]
    ppermute x14 -> x0, waiting for transfers between devices: 16.5 us -> none  [shifted(): lax.ppermute(value, axis, [(source, source + steps) for source in range(i...]
    dot_general x4 -> x0, matrix products: 13.6 us -> none  [the longest x2 9.27 us: local(): jnp.einsum('phl,kl->hpk', query_slots[slot], window, preferred_element_ty...]
    dynamic_slice x3 -> x0, local copies, waits for them, and re-layouts: 4.41 us -> none  [the longest x1 2.29 us: local(): lax.dynamic_slice_in_dim(source, jnp.clip(block, 0, 3 * WINDOW + 1) * spa...]
    concatenate x3 -> x0, local copies, waits for them, and re-layouts: 4.26 us -> none  [the longest x2 2.93 us: local(): window = jnp.concatenate(picked, axis=0)]
    unnamed x9 -> x2, local copies, waits for them, and re-layouts: 4.75 us -> 1.19 us
  transfers between devices with their start and end apart: 14 -> 0, of which waited for: 3 -> 0; matrix products, arithmetic and copies ran while one was open for 3% -> 0% of each run, Pallas kernels for 0% -> 0%
where the time goes in v1:
time: 41.2 us; the launch traced here: 41 us
  Pallas kernels  39 us (95%)
  local copies, waits for them, and re-layouts  1.19 us (3%)
  other arithmetic  0.73 us (2%)
    pallas_call x1, Pallas kernels, local(): pl.pallas_call(functools.partial(gather_kernel, n, span), out_shape=jax.S...  21.1 us
    pallas_call x1, Pallas kernels, local(): pl.pallas_call(functools.partial(attend_kernel, n, span, heads), out_shap...  17.9 us
    unnamed x2, local copies, waits for them, and re-layouts  1.19 us

profile of v1, /device:TPU:1, one launch (start us, length us, event | category | flops | bytes accessed | tf_op | source)
XLA Modules:
  0.0 41.0 jit_solution(14531650117156131196)
XLA Ops:
  0.0 0.7 %pad_add_fusion.order_ref = s32[33]{0:T(128)S(1)} fusion(s32[1]{0:T(128)} %bitcast, s32[32]{0:T(128)} %order_ref.1), kind=kLoop, calls=%fused_computation | loop fusion | flops 33 | bytes 264 | tf_op jit(solution)/shard_map/concatenate | solution.py:145
  0.7 21.1 %gather_windows.1.win_ref = bf16[2,384,576]{2,1,0:T(8,128)(2,1)} custom-call(s32[32]{0:T(128)} %order_ref.1, bf16[96,576]{1,0:T(8,128)(2,1)} %kv_ref.1), custom_call_target="tpu_custom_call" | custom-call | tf_op jit(solution)/shard_map/gather_windows/pallas_call | solution.py:130
  21.9 0.0 copy-start
  21.9 1.2 %copy-done = bf16[2,384,576]{2,1,0:T(8,128)(2,1)S(1)} copy-done((bf16[2,384,576]{2,1,0:T(8,128)(2,1)S(1)}, bf16[2,384,576]{2,1,0:T(8,128)(2,1)}, u32[]{:S(2)}) %copy-start) | copy-done | bytes 884760
  23.1 17.9 %attend.1 = bf16[96,32768]{1,0:T(8,128)(2,1)} custom-call(s32[33]{0:T(128)S(1)} %pad_add_fusion.order_ref, bf16[96,64,576]{2,1,0:T(8,128)(2,1)} %q_ref.1, bf16[2,384,576]{2,1,0:T(8,128)(2,1)S(1)} %copy-done), custom_call_target="tpu_custom_call" | custom-call | tf_op jit(solution)/shard_map/attend/pallas_call | solution.py:150
Async XLA Ops:
  21.9 1.2 %copy-start = (bf16[2,384,576]{2,1,0:T(8,128)(2,1)S(1)}, bf16[2,384,576]{2,1,0:T(8,128)(2,1)}, u32[]{:S(2)}) copy-start(bf16[2,384,576]{2,1,0:T(8,128)(2,1)} %gather_windows.1.win_ref) | copy-start | bytes 2654212

commit v2 on v1

v2 whole, which is shorter than its diff:
```python
import functools

import jax
import jax.numpy as jnp
from jax import lax
from jax.experimental import pallas as pl
from jax.experimental.pallas import tpu as pltpu
from jax.sharding import PartitionSpec as P

KEY_DIM = 128
ROPE_DIM = 64
LATENT = 512
WINDOW = 7
HEAD_BLOCK = 16
PITCH = 17
PARTS = 2
LOG2E = 1.4426950408889634
MESH = pl.DeviceIdType.MESH


def gather_kernel(n, span, order_ref, kv_ref, win_ref, mine, send_lo, send_hi, send_x, send_f, recv_sem):
    me = lax.axis_index("ctx")
    last = 2 * n - 1

    barrier = pltpu.get_barrier_semaphore()
    for k in range(1, WINDOW + 1):
        for other, ok in ((me + k, me + k < n), (me - k, me >= k)):
            @pl.when(ok)
            def _():
                pl.semaphore_signal(barrier, inc=1, device_id={"ctx": other}, device_id_type=MESH)

    first, second = kv_ref[:span], kv_ref[span:]
    lower_first = jnp.full(first.shape, order_ref[2 * me], jnp.int32) < n
    own_lower = jnp.where(lower_first, first, second)
    own_upper = jnp.where(lower_first, second, first)
    mine[0] = own_lower
    mine[1] = own_upper
    own_rows = pl.ds(WINDOW * span, span)
    pl.semaphore_wait(barrier, jnp.minimum(me, WINDOW) + jnp.minimum(n - 1 - me, WINDOW))

    def rows(back):
        return pl.ds(pl.multiple_of((WINDOW - back) * span, 16), span)

    def copy(which, target, window, back, send):
        return pltpu.make_async_remote_copy(
            src_ref=mine.at[which],
            dst_ref=win_ref.at[window, rows(back)],
            send_sem=send,
            recv_sem=recv_sem.at[window, back],
            device_id={"ctx": target},
            device_id_type=MESH,
        )

    even = me % 2 == 0
    sibling = me + 1 - 2 * (me % 2)

    def sends(action):
        for k in (6, 4, 7, 2, 1):
            up, down = me + k < n, me >= k
            if k == 7:
                up, down = up & (me % 2 == 1), down & even
            if k == 1:
                up, down = up & even, down & (me % 2 == 1)

            @pl.when(up)
            def _():
                action(copy(0, me + k, 0, k, send_lo.at[k]))

            @pl.when(down)
            def _():
                action(copy(1, me - k, 1, k, send_hi.at[k]))

        for k in range(1, WINDOW + 1):
            back = last - 2 * me + k

            @pl.when((me >= k) & (back <= WINDOW))
            def _():
                action(copy(0, me - k, 1, back, send_x.at[k]))

    def relay(window, k):
        back = k + 1 - 2 * (me % 2) if window == 0 else k - 1 + 2 * (me % 2)
        return pltpu.make_async_remote_copy(
            src_ref=win_ref.at[window, rows(k)],
            dst_ref=win_ref.at[window, rows(back)],
            send_sem=send_f.at[window, k],
            recv_sem=recv_sem.at[window, back],
            device_id={"ctx": sibling},
            device_id_type=MESH,
        )

    def arrived(window, k):
        copy(0, sibling, window, k, send_lo.at[k]).wait_recv()

    sends(lambda c: c.start())
    win_ref[0, own_rows] = own_lower
    win_ref[1, own_rows] = own_upper
    for k in (2, 4, 6):
        for window, ok in ((0, me >= k), (1, me + k < n)):
            @pl.when(ok)
            def _():
                arrived(window, k)
                relay(window, k).start()

    for k in range(1, WINDOW + 1):
        if k % 2:
            @pl.when(me >= k)
            def _():
                arrived(0, k)

        @pl.when(me < k)
        def _():
            win_ref[0, rows(k)] = jnp.zeros_like(own_lower)

    for k in range(1, WINDOW + 1):
        @pl.when((2 * me + k < last) & (me + k >= n) if k in (2, 4, 6) else 2 * me + k < last)
        def _():
            arrived(1, k)

        @pl.when(2 * me + k >= last)
        def _():
            win_ref[1, rows(k)] = win_ref[0, rows(2 * me + k - last)]
    sends(lambda c: c.wait_send())
    for k in (2, 4, 6):
        for window, ok in ((0, me >= k), (1, me + k < n)):
            @pl.when(ok)
            def _():
                relay(window, k).wait_send()


def attend_kernel(n, span, heads, order_ref, q_hbm, win_ref, out_hbm, q, out, scores, bias, probs, q_sem, out_sem):
    me = lax.axis_index("ctx")
    width = (WINDOW + 1) * span
    groups = heads // HEAD_BLOCK
    blocks = 2 * groups
    chunks = width // 128
    factor = LOG2E * (KEY_DIM + ROPE_DIM) ** -0.5
    columns = HEAD_BLOCK * LATENT

    def multiple(value, of):
        return value if isinstance(value, int) else pl.multiple_of(value, of)

    def q_copy(b):
        slot, group = b // groups, b % groups
        positions = pl.ds(multiple(slot * span, 16), span)
        block_heads = pl.ds(multiple(group * HEAD_BLOCK, HEAD_BLOCK), HEAD_BLOCK)
        return pltpu.make_async_copy(q_hbm.at[positions, block_heads], q.at[b], q_sem.at[b])

    def out_copy(b):
        slot, group = b // groups, b % groups
        positions = pl.ds(multiple(slot * span, 16), span)
        return pltpu.make_async_copy(
            out.at[b], out_hbm.at[positions, pl.ds(multiple(group * columns, columns), columns)], out_sem.at[b]
        )

    for b in range(blocks):
        q_copy(b).start()
    for slot in range(2):
        span_id = order_ref[2 * me + slot]
        keypos = lax.broadcasted_iota(jnp.int32, (span, width), 1)
        row = lax.broadcasted_iota(jnp.int32, (span, width), 0)
        allowed = (keypos >= (WINDOW - span_id) * span) & (keypos - WINDOW * span <= row)
        bias[slot] = jnp.where(allowed, 0.0, -1e30)

    def window_of(b):
        return jnp.where(order_ref[2 * me + b // groups] < n, 0, 1)

    pos_part, head_part = span // PARTS, HEAD_BLOCK // PARTS

    def score(b, parity, part):
        block = q[b, part * pos_part : (part + 1) * pos_part].reshape(pos_part * HEAD_BLOCK, q.shape[3])
        product = lax.dot_general(
            block, win_ref[window_of(b)], (((1,), (1,)), ((), ())), preferred_element_type=jnp.float32
        )
        for c in range(chunks):
            for p in range(pos_part):
                first = (part * pos_part + p) * PITCH
                scores[parity * chunks + c, first : first + HEAD_BLOCK] = product[
                    p * HEAD_BLOCK : (p + 1) * HEAD_BLOCK, c * 128 : (c + 1) * 128
                ]

    def mix(b, parity, part):
        for h in range(part * head_part, (part + 1) * head_part):
            tiles = [
                scores.at[parity * chunks + c][pl.ds(h, span, stride=PITCH), :]
                + bias[b // groups, :, c * 128 : (c + 1) * 128]
                for c in range(chunks)
            ]
            largest = jnp.max(functools.reduce(jnp.maximum, tiles), axis=-1, keepdims=True)
            weights = [jnp.exp2((tile - largest) * factor) for tile in tiles]
            inverse = 1.0 / jnp.sum(sum(weights), axis=-1, keepdims=True)
            for c in range(chunks):
                probs[parity, h * span : (h + 1) * span, c * 128 : (c + 1) * 128] = (weights[c] * inverse).astype(
                    jnp.bfloat16
                )
        rows = head_part * span
        mixed = jnp.dot(
            probs[parity, part * rows : (part + 1) * rows],
            win_ref[window_of(b), :, :LATENT],
            preferred_element_type=jnp.float32,
        )
        for k in range(head_part):
            h = part * head_part + k
            out[b, :, h * LATENT : (h + 1) * LATENT] = mixed[k * span : (k + 1) * span].astype(jnp.bfloat16)

    def step(b, parity, more=True):
        if more:
            q_copy(b + 1).wait()
        for part in range(PARTS):
            if more:
                score(b + 1, 1 - parity, part)
            mix(b, parity, part)
        out_copy(b).start()

    q_copy(0).wait()
    for part in range(PARTS):
        score(0, 0, part)

    @pl.loop(0, groups - 1)
    def _(pair):
        step(2 * pair, 0)
        step(2 * pair + 1, 1)

    step(blocks - 2, 0)
    step(blocks - 1, 1, more=False)
    for b in range(blocks):
        out_copy(b).wait()


def local(queries, kv_latent, span_order):
    n = lax.axis_size("ctx")
    tokens, heads, dim = queries.shape
    span = tokens // 2
    width = (WINDOW + 1) * span
    windows = pl.pallas_call(
        functools.partial(gather_kernel, n, span),
        out_shape=jax.ShapeDtypeStruct((2, width, dim), jnp.bfloat16),
        in_specs=[pl.BlockSpec(memory_space=pltpu.SMEM), pl.BlockSpec(memory_space=pltpu.VMEM)],
        out_specs=pl.BlockSpec(memory_space=pltpu.VMEM),
        scratch_shapes=[
            pltpu.VMEM((2, span, dim), jnp.bfloat16),
            pltpu.SemaphoreType.DMA((WINDOW + 1,)),
            pltpu.SemaphoreType.DMA((WINDOW + 1,)),
            pltpu.SemaphoreType.DMA((WINDOW + 1,)),
            pltpu.SemaphoreType.DMA((2, WINDOW + 1)),
            pltpu.SemaphoreType.DMA((2, WINDOW + 1)),
        ],
        compiler_params=pltpu.CompilerParams(collective_id=0, has_side_effects=True),
        name="gather_windows",
    )(span_order, kv_latent)
    blocks = 2 * (heads // HEAD_BLOCK)
    return pl.pallas_call(
        functools.partial(attend_kernel, n, span, heads),
        out_shape=jax.ShapeDtypeStruct((tokens, heads * LATENT), jnp.bfloat16),
        in_specs=[
            pl.BlockSpec(memory_space=pltpu.SMEM),
            pl.BlockSpec(memory_space=pl.ANY),
            pl.BlockSpec(memory_space=pltpu.VMEM),
        ],
        out_specs=pl.BlockSpec(memory_space=pl.ANY),
        scratch_shapes=[
            pltpu.VMEM((blocks, span, HEAD_BLOCK, dim), jnp.bfloat16),
            pltpu.VMEM((blocks, span, HEAD_BLOCK * LATENT), jnp.bfloat16),
            pltpu.VMEM((2 * (width // 128), span * PITCH, 128), jnp.float32),
            pltpu.VMEM((2, span, width), jnp.float32),
            pltpu.VMEM((2, span * HEAD_BLOCK, width), jnp.bfloat16),
            pltpu.SemaphoreType.DMA((blocks,)),
            pltpu.SemaphoreType.DMA((blocks,)),
        ],
        compiler_params=pltpu.CompilerParams(vmem_limit_bytes=48 * 1024 * 1024),
        name="attend",
    )(span_order, queries, windows)


def solution(mesh):
    in_specs = (P(("groups", "ctx"), None, None), P(("groups", "ctx"), None), P("groups"))
    out_specs = P(("groups", "ctx"), None)
    return jax.shard_map(local, mesh=mesh, in_specs=in_specs, out_specs=out_specs, check_vma=False)
```

time: 41.2 us -> 30.7 us (0.75)
  the two profiles are of different devices: /device:TPU:1 before, /device:TPU:13 now
where the time goes in v2:
time: 30.7 us; the launch traced here: 30.6 us
  Pallas kernels  28.7 us (93%)
  local copies, waits for them, and re-layouts  1.85 us (6%)
    pallas_call x1, Pallas kernels, local(): pl.pallas_call(functools.partial(gather_kernel, n, span), out_shape=jax.S...  15.8 us
    pallas_call x1, Pallas kernels, local(): pl.pallas_call(functools.partial(attend_kernel, n, span, heads), out_shap...  12.9 us
    unnamed x4, local copies, waits for them, and re-layouts  1.85 us

profile of v2, /device:TPU:13, one launch (start us, length us, event | category | flops | bytes accessed | tf_op | source)
XLA Modules:
  0.0 30.6 jit_solution(6498603711424234253)
XLA Ops:
  0.0 15.8 %gather_windows.1.win_ref = bf16[2,384,576]{2,1,0:T(8,128)(2,1)} custom-call(s32[32]{0:T(128)} %order_ref.3, bf16[96,576]{1,0:T(8,128)(2,1)} %kv_ref.1), custom_call_target="tpu_custom_call" | custom-call | tf_op jit(solution)/shard_map/gather_windows/pallas_call | solution.py:234
  15.8 0.0 copy-start
  15.8 1.2 %copy-done = bf16[2,384,576]{2,1,0:T(8,128)(2,1)S(1)} copy-done((bf16[2,384,576]{2,1,0:T(8,128)(2,1)S(1)}, bf16[2,384,576]{2,1,0:T(8,128)(2,1)}, u32[]{:S(2)}) %copy-start) | copy-done | bytes 884760
  17.0 0.0 copy-start.1
  17.0 0.7 %copy-done.1 = s32[32]{0:T(128)S(1)} copy-done((s32[32]{0:T(128)S(1)}, s32[32]{0:T(128)}, u32[]{:S(2)}) %copy-start.1) | copy-done | bytes 152
  17.7 12.9 %attend.1 = bf16[96,32768]{1,0:T(8,128)(2,1)} custom-call(s32[32]{0:T(128)S(1)} %copy-done.1, bf16[96,64,576]{2,1,0:T(8,128)(2,1)} %q_hbm.1, bf16[2,384,576]{2,1,0:T(8,128)(2,1)S(1)} %copy-done), custom_call_target="tpu_custom_call" | custom-call | tf_op jit(solution)/shard_map/attend/pallas_call | solution.py:251
Async XLA Ops:
  15.8 1.2 %copy-start = (bf16[2,384,576]{2,1,0:T(8,128)(2,1)S(1)}, bf16[2,384,576]{2,1,0:T(8,128)(2,1)}, u32[]{:S(2)}) copy-start(bf16[2,384,576]{2,1,0:T(8,128)(2,1)} %gather_windows.1.win_ref) | copy-start | bytes 2654212
  17.0 0.7 %copy-start.1 = (s32[32]{0:T(128)S(1)}, s32[32]{0:T(128)}, u32[]{:S(2)}) copy-start(s32[32]{0:T(128)} %order_ref.3) | copy-start | bytes 388

commit v3 on v2

--- a/solution.py
+++ b/solution.py
@@ -18,9 +18,23 @@
 MESH = pl.DeviceIdType.MESH
 
 
-def gather_kernel(n, span, order_ref, kv_ref, win_ref, mine, send_lo, send_hi, send_x, send_f, recv_sem):
+def gather_kernel(
+    n, span, order_ref, kv_ref, q_hbm, win_ref, near_ref, mine, near_keys, q, send_lo, send_hi, send_x, send_f, recv_sem, q_sem
+):
     me = lax.axis_index("ctx")
     last = 2 * n - 1
+
+    groups = q_hbm.shape[1] // HEAD_BLOCK
+    blocks = 2 * groups
+
+    def q_copy(b):
+        slot, group = b // groups, b % groups
+        return pltpu.make_async_copy(
+            q_hbm.at[pl.ds(slot * span, span), pl.ds(group * HEAD_BLOCK, HEAD_BLOCK)], q.at[b], q_sem.at[b]
+        )
+
+    for b in range(blocks):
+        q_copy(b).start()
 
     barrier = pltpu.get_barrier_semaphore()
     for k in range(1, WINDOW + 1):
@@ -55,7 +69,7 @@
     sibling = me + 1 - 2 * (me % 2)
 
     def sends(action):
-        for k in (6, 4, 7, 2, 1):
+        for k in (2, 1, 6, 4, 7):
             up, down = me + k < n, me >= k
             if k == 7:
                 up, down = up & (me % 2 == 1), down & even
@@ -94,31 +108,59 @@
     sends(lambda c: c.start())
     win_ref[0, own_rows] = own_lower
     win_ref[1, own_rows] = own_upper
-    for k in (2, 4, 6):
+    def pass_on(k):
         for window, ok in ((0, me >= k), (1, me + k < n)):
             @pl.when(ok)
             def _():
                 arrived(window, k)
                 relay(window, k).start()
 
-    for k in range(1, WINDOW + 1):
-        if k % 2:
-            @pl.when(me >= k)
-            def _():
-                arrived(0, k)
-
-        @pl.when(me < k)
-        def _():
-            win_ref[0, rows(k)] = jnp.zeros_like(own_lower)
-
-    for k in range(1, WINDOW + 1):
-        @pl.when((2 * me + k < last) & (me + k >= n) if k in (2, 4, 6) else 2 * me + k < last)
-        def _():
-            arrived(1, k)
-
-        @pl.when(2 * me + k >= last)
-        def _():
-            win_ref[1, rows(k)] = win_ref[0, rows(2 * me + k - last)]
+    def finish(ks):
+        for k in ks:
+            if k % 2:
+                @pl.when(me >= k)
+                def _():
+                    arrived(0, k)
+
+            @pl.when(me < k)
+            def _():
+                win_ref[0, rows(k)] = jnp.zeros_like(own_lower)
+
+        for k in ks:
+            @pl.when(((2 * me + k < last) & (me + k >= n)) if k % 2 == 0 else 2 * me + k < last)
+            def _():
+                arrived(1, k)
+
+        for k in ks:
+            @pl.when(2 * me + k >= last)
+            def _():
+                win_ref[1, rows(k)] = win_ref[0, rows(2 * me + k - last)]
+
+    def near_scores(lo, hi):
+        @pl.loop(lo, hi)
+        def _(b):
+            block = q[b].reshape(span * HEAD_BLOCK, q.shape[3])
+            product = lax.dot_general(
+                block, near_keys[b // groups], (((1,), (1,)), ((), ())), preferred_element_type=jnp.float32
+            )
+            for p in range(span):
+                near_ref[b, p * PITCH : p * PITCH + HEAD_BLOCK] = product[p * HEAD_BLOCK : (p + 1) * HEAD_BLOCK]
+
+    pass_on(2)
+    finish((1, 2))
+    tail = pl.ds(win_ref.shape[1] - 128, 128)
+    near_lower, near_upper = win_ref[0, tail], win_ref[1, tail]
+    lower_first = jnp.full(near_lower.shape, order_ref[2 * me], jnp.int32) < n
+    near_keys[0] = jnp.where(lower_first, near_lower, near_upper)
+    near_keys[1] = jnp.where(lower_first, near_upper, near_lower)
+    for b in range(blocks):
+        q_copy(b).wait()
+    near_scores(0, blocks // 4)
+    pass_on(4)
+    near_scores(blocks // 4, blocks // 2)
+    pass_on(6)
+    near_scores(blocks // 2, blocks)
+    finish((3, 4, 5, 6, 7))
     sends(lambda c: c.wait_send())
     for k in (2, 4, 6):
         for window, ok in ((0, me >= k), (1, me + k < n)):
@@ -127,7 +169,7 @@
                 relay(window, k).wait_send()
 
 
-def attend_kernel(n, span, heads, order_ref, q_hbm, win_ref, out_hbm, q, out, scores, bias, probs, q_sem, out_sem):
+def attend_kernel(n, span, heads, order_ref, q_hbm, win_ref, near_ref, out_hbm, q, out, scores, bias, probs, q_sem, out_sem):
     me = lax.axis_index("ctx")
     width = (WINDOW + 1) * span
     groups = heads // HEAD_BLOCK
@@ -169,21 +211,21 @@
     def score(b, parity, part):
         block = q[b, part * pos_part : (part + 1) * pos_part].reshape(pos_part * HEAD_BLOCK, q.shape[3])
         product = lax.dot_general(
-            block, win_ref[window_of(b)], (((1,), (1,)), ((), ())), preferred_element_type=jnp.float32
-        )
-        for c in range(chunks):
+            block, win_ref[window_of(b), : width - 128], (((1,), (1,)), ((), ())), preferred_element_type=jnp.float32
+        )
+        for c in range(chunks - 1):
             for p in range(pos_part):
                 first = (part * pos_part + p) * PITCH
-                scores[parity * chunks + c, first : first + HEAD_BLOCK] = product[
+                scores[parity * (chunks - 1) + c, first : first + HEAD_BLOCK] = product[
                     p * HEAD_BLOCK : (p + 1) * HEAD_BLOCK, c * 128 : (c + 1) * 128
                 ]
 
     def mix(b, parity, part):
         for h in range(part * head_part, (part + 1) * head_part):
+            planes = [scores.at[parity * (chunks - 1) + c] for c in range(chunks - 1)] + [near_ref.at[b]]
             tiles = [
-                scores.at[parity * chunks + c][pl.ds(h, span, stride=PITCH), :]
-                + bias[b // groups, :, c * 128 : (c + 1) * 128]
-                for c in range(chunks)
+                plane[pl.ds(h, span, stride=PITCH), :] + bias[b // groups, :, c * 128 : (c + 1) * 128]
+                for c, plane in enumerate(planes)
             ]
             largest = jnp.max(functools.reduce(jnp.maximum, tiles), axis=-1, keepdims=True)
             weights = [jnp.exp2((tile - largest) * factor) for tile in tiles]
@@ -231,36 +273,49 @@
     tokens, heads, dim = queries.shape
     span = tokens // 2
     width = (WINDOW + 1) * span
-    windows = pl.pallas_call(
+    blocks = 2 * (heads // HEAD_BLOCK)
+    windows, near = pl.pallas_call(
         functools.partial(gather_kernel, n, span),
-        out_shape=jax.ShapeDtypeStruct((2, width, dim), jnp.bfloat16),
-        in_specs=[pl.BlockSpec(memory_space=pltpu.SMEM), pl.BlockSpec(memory_space=pltpu.VMEM)],
-        out_specs=pl.BlockSpec(memory_space=pltpu.VMEM),
+        out_shape=(
+            jax.ShapeDtypeStruct((2, width, dim), jnp.bfloat16),
+            jax.ShapeDtypeStruct((blocks, span * PITCH, 128), jnp.float32),
+        ),
+        in_specs=[
+            pl.BlockSpec(memory_space=pltpu.SMEM),
+            pl.BlockSpec(memory_space=pltpu.VMEM),
+            pl.BlockSpec(memory_space=pltpu.HBM),
+        ],
+        out_specs=(pl.BlockSpec(memory_space=pltpu.VMEM), pl.BlockSpec(memory_space=pltpu.VMEM)),
         scratch_shapes=[
             pltpu.VMEM((2, span, dim), jnp.bfloat16),
+            pltpu.VMEM((2, 128, dim), jnp.bfloat16),
+            pltpu.VMEM((blocks, span, HEAD_BLOCK, dim), jnp.bfloat16),
             pltpu.SemaphoreType.DMA((WINDOW + 1,)),
             pltpu.SemaphoreType.DMA((WINDOW + 1,)),
             pltpu.SemaphoreType.DMA((WINDOW + 1,)),
             pltpu.SemaphoreType.DMA((2, WINDOW + 1)),
             pltpu.SemaphoreType.DMA((2, WINDOW + 1)),
+            pltpu.SemaphoreType.DMA((blocks,)),
         ],
-        compiler_params=pltpu.CompilerParams(collective_id=0, has_side_effects=True),
+        compiler_params=pltpu.CompilerParams(
+            collective_id=0, has_side_effects=True, vmem_limit_bytes=48 * 1024 * 1024
+        ),
         name="gather_windows",
-    )(span_order, kv_latent)
-    blocks = 2 * (heads // HEAD_BLOCK)
+    )(span_order, kv_latent, queries)
     return pl.pallas_call(
         functools.partial(attend_kernel, n, span, heads),
         out_shape=jax.ShapeDtypeStruct((tokens, heads * LATENT), jnp.bfloat16),
         in_specs=[
             pl.BlockSpec(memory_space=pltpu.SMEM),
-            pl.BlockSpec(memory_space=pl.ANY),
+            pl.BlockSpec(memory_space=pltpu.HBM),
+            pl.BlockSpec(memory_space=pltpu.VMEM),
             pl.BlockSpec(memory_space=pltpu.VMEM),
         ],
-        out_specs=pl.BlockSpec(memory_space=pl.ANY),
+        out_specs=pl.BlockSpec(memory_space=pltpu.HBM),
         scratch_shapes=[
             pltpu.VMEM((blocks, span, HEAD_BLOCK, dim), jnp.bfloat16),
             pltpu.VMEM((blocks, span, HEAD_BLOCK * LATENT), jnp.bfloat16),
-            pltpu.VMEM((2 * (width // 128), span * PITCH, 128), jnp.float32),
+            pltpu.VMEM((2 * (width // 128 - 1), span * PITCH, 128), jnp.float32),
             pltpu.VMEM((2, span, width), jnp.float32),
             pltpu.VMEM((2, span * HEAD_BLOCK, width), jnp.bfloat16),
             pltpu.SemaphoreType.DMA((blocks,)),
@@ -268,7 +323,7 @@
         ],
         compiler_params=pltpu.CompilerParams(vmem_limit_bytes=48 * 1024 * 1024),
         name="attend",
-    )(span_order, queries, windows)
+    )(span_order, queries, windows, near)
 
 
 def solution(mesh):

time: 30.7 us -> 30 us (0.977); the launches traced: 30.6 us -> 29.5 us
  Pallas kernels: 28.7 us -> 27.9 us
    pallas_call x1, Pallas kernels: 12.9 us -> 12.3 us  [local(): pl.pallas_call(functools.partial(attend_kernel, n, span, heads), out_shap...]
where the time goes in v3:
time: 30 us; the launch traced here: 29.5 us
  Pallas kernels  27.9 us (93%)
  local copies, waits for them, and re-layouts  1.56 us (5%)
    pallas_call x1, Pallas kernels, local(): pl.pallas_call(functools.partial(gather_kernel, n, span), out_shape=(jax....  15.6 us
    pallas_call x1, Pallas kernels, local(): pl.pallas_call(functools.partial(attend_kernel, n, span, heads), out_shap...  12.3 us
    unnamed x4, local copies, waits for them, and re-layouts  1.56 us

profile of v3, /device:TPU:13, one launch (start us, length us, event | category | flops | bytes accessed | tf_op | source)
XLA Modules:
  0.0 29.5 jit_solution(10503786967630466846)
XLA Ops:
  0.0 0.0 copy-start
  0.0 0.9 %copy-done = bf16[96,576]{1,0:T(8,128)(2,1)S(1)} copy-done((bf16[96,576]{1,0:T(8,128)(2,1)S(1)}, bf16[96,576]{1,0:T(8,128)(2,1)}, u32[]{:S(2)}) %copy-start) | copy-done | bytes 110616
  0.9 0.0 copy-start.1
  0.9 0.7 %copy-done.1 = s32[32]{0:T(128)S(1)} copy-done((s32[32]{0:T(128)S(1)}, s32[32]{0:T(128)}, u32[]{:S(2)}) %copy-start.1) | copy-done | bytes 152
  1.6 15.6 %gather_windows.1 = (bf16[2,384,576]{2,1,0:T(8,128)(2,1)S(1)}, f32[8,816,128]{2,1,0:T(8,128)S(1)}) custom-call(s32[32]{0:T(128)S(1)} %copy-done.1, bf16[96,576]{1,0:T(8,128)(2,1)S(1)} %copy-done, bf16[96,64,576]{2,1,0:T(8,128)(2,1)} %q_hbm.3), custom_call_target="tpu_custom_call" | custom-call | tf_op jit(solution)/shard_map/gather_windows/pallas_call | solution.py:277
  17.2 12.3 %attend.1 = bf16[96,32768]{1,0:T(8,128)(2,1)} custom-call(s32[32]{0:T(128)S(1)} %copy-done.1, bf16[96,64,576]{2,1,0:T(8,128)(2,1)} %q_hbm.3, bf16[2,384,576]{2,1,0:T(8,128)(2,1)S(1)} %get-tuple-element.7.win_ref, f32[8,816,128]{2,1,0:T(8,128)S(1)} %get-tuple-element.8.near_ref), custom_call_target="tpu_custom_call" | custom-call | tf_op jit(solution)/shard_map/attend/pallas_call | solution.py:305
Async XLA Ops:
  0.0 0.9 %copy-start = (bf16[96,576]{1,0:T(8,128)(2,1)S(1)}, bf16[96,576]{1,0:T(8,128)(2,1)}, u32[]{:S(2)}) copy-start(bf16[96,576]{1,0:T(8,128)(2,1)} %kv_ref.1) | copy-start | bytes 331780
  0.9 0.7 %copy-start.1 = (s32[32]{0:T(128)S(1)}, s32[32]{0:T(128)}, u32[]{:S(2)}) copy-start(s32[32]{0:T(128)} %order_ref.3) | copy-start | bytes 388

commit v4 on v3

--- a/solution.py
+++ b/solution.py
@@ -155,11 +155,10 @@
     near_keys[1] = jnp.where(lower_first, near_upper, near_lower)
     for b in range(blocks):
         q_copy(b).wait()
+    pass_on(4)
     near_scores(0, blocks // 4)
-    pass_on(4)
-    near_scores(blocks // 4, blocks // 2)
     pass_on(6)
-    near_scores(blocks // 2, blocks)
+    near_scores(blocks // 4, blocks)
     finish((3, 4, 5, 6, 7))
     sends(lambda c: c.wait_send())
     for k in (2, 4, 6):

time: 30 us -> 30 us (level)
  no operation moved by 1% of the time
where the time goes in v4:
time: 30 us; the launch traced here: 29.5 us
  Pallas kernels  27.9 us (93%)
  local copies, waits for them, and re-layouts  1.56 us (5%)
    pallas_call x1, Pallas kernels, local(): pl.pallas_call(functools.partial(gather_kernel, n, span), out_shape=(jax....  15.6 us
    pallas_call x1, Pallas kernels, local(): pl.pallas_call(functools.partial(attend_kernel, n, span, heads), out_shap...  12.3 us
    unnamed x4, local copies, waits for them, and re-layouts  1.56 us

profile of v4, /device:TPU:13, one launch (start us, length us, event | category | flops | bytes accessed | tf_op | source)
XLA Modules:
  0.0 29.5 jit_solution(18016468979474801630)
XLA Ops:
  0.0 0.0 copy-start
  0.0 0.9 %copy-done = bf16[96,576]{1,0:T(8,128)(2,1)S(1)} copy-done((bf16[96,576]{1,0:T(8,128)(2,1)S(1)}, bf16[96,576]{1,0:T(8,128)(2,1)}, u32[]{:S(2)}) %copy-start) | copy-done | bytes 110616
  0.9 0.0 copy-start.1
  0.9 0.7 %copy-done.1 = s32[32]{0:T(128)S(1)} copy-done((s32[32]{0:T(128)S(1)}, s32[32]{0:T(128)}, u32[]{:S(2)}) %copy-start.1) | copy-done | bytes 152
  1.6 15.6 %gather_windows.1 = (bf16[2,384,576]{2,1,0:T(8,128)(2,1)S(1)}, f32[8,816,128]{2,1,0:T(8,128)S(1)}) custom-call(s32[32]{0:T(128)S(1)} %copy-done.1, bf16[96,576]{1,0:T(8,128)(2,1)S(1)} %copy-done, bf16[96,64,576]{2,1,0:T(8,128)(2,1)} %q_hbm.3), custom_call_target="tpu_custom_call" | custom-call | tf_op jit(solution)/shard_map/gather_windows/pallas_call | solution.py:276
  17.2 12.3 %attend.1 = bf16[96,32768]{1,0:T(8,128)(2,1)} custom-call(s32[32]{0:T(128)S(1)} %copy-done.1, bf16[96,64,576]{2,1,0:T(8,128)(2,1)} %q_hbm.3, bf16[2,384,576]{2,1,0:T(8,128)(2,1)S(1)} %get-tuple-element.7.win_ref, f32[8,816,128]{2,1,0:T(8,128)S(1)} %get-tuple-element.8.near_ref), custom_call_target="tpu_custom_call" | custom-call | tf_op jit(solution)/shard_map/attend/pallas_call | solution.py:304
Async XLA Ops:
  0.0 0.9 %copy-start = (bf16[96,576]{1,0:T(8,128)(2,1)S(1)}, bf16[96,576]{1,0:T(8,128)(2,1)}, u32[]{:S(2)}) copy-start(bf16[96,576]{1,0:T(8,128)(2,1)} %kv_ref.1) | copy-start | bytes 331780
  0.9 0.7 %copy-start.1 = (s32[32]{0:T(128)S(1)}, s32[32]{0:T(128)}, u32[]{:S(2)}) copy-start(s32[32]{0:T(128)} %order_ref.3) | copy-start | bytes 388
